TPU v7x, 32 devices: a whole 2x2x4 slice. The times are simulated.
32 devices in a mesh: groups: 2 (over y), docs: 4 (over z), feat: 2 (over x), rep: 2 (over core).
Axes of the slice: x: 2, y: 2, z: 4, core: 2. Of those that a mesh axis runs over, the one named last changes fastest.
Arguments:
- activations: bfloat16 [8192, 8192], P(('groups', 'docs', 'rep'), 'feat'), parts along dimension 0, may hold values from -6 to 6
- out_grads: bfloat16 [8192, 8192], P(('groups', 'docs', 'rep'), 'feat'), parts along dimension 0, may hold values from -6 to 6
- proj_in: bfloat16 [8192, 128], P('feat'), may hold values from -0.0625 to 0.0625
- proj_out: bfloat16 [8192, 128], P('feat'), may hold values from -0.0625 to 0.0625
- inv_in: float32 [128, 128], replicated, may hold values from -0.5 to 2.5, as said below
- inv_out: float32 [128, 128], replicated, may hold values from -0.5 to 2.5, as said below
- segment_ids: int32 [8192], P(('groups', 'docs', 'rep')), parts along dimension 0, may hold values from 0 to 511, never falling along the last dimension, each value on 1 to 32 neighbouring positions
- owner_map: int32 [1024], P('groups'), parts along dimension 0, may hold values from 0 to 511
- stored: bfloat16 [4096, 16384], P(('groups', 'docs'), 'feat'), parts along dimension 0, may hold values from -0.005859375 to 0.005859375
Outputs:
- scores: float32 [1024, 2048], P(('groups', 'rep'), ('docs', 'feat')), parts along dimension 0
There are 2 independent parts, one for each index of `groups`. A program takes and returns all parts, laid end to end along the dimension named above; an argument that names none is the same for every part. Nothing has to cross between parts.
Inputs may be any that keep to these rules, and one draw needn't show every extreme that they name: `inv_in`: symmetric. `inv_out`: symmetric. `segment_ids`: never falling along the tokens; each segment has 1 to 32 tokens, one exactly 32.
All inputs are finite; a program needn't handle non-finite values.
Results may differ from a plain program's by a relative error of at most 0.01.
Values may be sent and summed in bfloat16 or wider, within the bound.
A program may use at most 64 MiB of HBM per device.

v0:
```python
import jax
import jax.numpy as jnp
from jax import lax
from jax.sharding import PartitionSpec as P

QUERIES = 512


def outer_rows(side_g, side_x):
    count = side_g.shape[0]
    joined = side_g[:, :, None] * side_x[:, None, :]
    return joined.reshape(count, side_g.shape[1] * side_x.shape[1]).astype(jnp.bfloat16)


def score_rows(panel_rows, stored):
    return lax.dot_general(
        panel_rows, stored, (((1,), (1,)), ((), ())), preferred_element_type=jnp.float32
    )


def on_device(
    activations, out_grads, proj_in, proj_out, inv_in, inv_out, segment_ids, owner_map, stored
):
    highest = lax.Precision.HIGHEST
    width_r = inv_in.shape[0]
    slice_count = lax.axis_size("feat")
    slice_rows = width_r // slice_count
    part_in = jnp.dot(activations, proj_in, preferred_element_type=jnp.float32)
    part_out = jnp.dot(out_grads, proj_out, preferred_element_type=jnp.float32)
    summed_in, summed_out = lax.psum((part_in, part_out), "feat")
    cond_x = jnp.dot(summed_in, inv_in, precision=highest, preferred_element_type=jnp.float32)
    cond_all = jnp.dot(summed_out, inv_out, precision=highest, preferred_element_type=jnp.float32)
    cond_g = lax.dynamic_slice_in_dim(cond_all, lax.axis_index("feat") * slice_rows, slice_rows, 1)
    products = outer_rows(cond_g, cond_x)
    seg_count = owner_map.shape[0]
    matches = segment_ids[:, None] == jnp.arange(seg_count, dtype=jnp.int32)[None, :]
    tok_query = jnp.sum(jnp.where(matches, owner_map[None, :], 0), axis=1)
    shard_count = lax.axis_size("docs")
    copies = lax.axis_size("rep")
    half_queries = QUERIES // copies
    block_queries = half_queries // shard_count
    target = (
        tok_query % half_queries // block_queries * (copies * block_queries)
        + tok_query // half_queries * block_queries
        + tok_query % block_queries
    )
    onehot = (target[:, None] == jnp.arange(QUERIES, dtype=jnp.int32)[None, :]).astype(jnp.bfloat16)
    partial_value = lax.dot_general(
        onehot, products, (((0,), (0,)), ((), ())), preferred_element_type=jnp.float32
    )
    rounded = lax.optimization_barrier(partial_value.astype(jnp.bfloat16))
    partial_terms = rounded.astype(jnp.float32)
    blocks = lax.psum_scatter(
        partial_terms.astype(jnp.bfloat16), ("docs", "rep"), scatter_dimension=0, tiled=True
    )
    partial_scores = score_rows(lax.all_gather(blocks, "docs", axis=0, tiled=True), stored)
    return lax.psum_scatter(partial_scores, "feat", scatter_dimension=1, tiled=True)


def solution(mesh):
    placed = (
        P(("groups", "docs", "rep"), "feat"),
        P(("groups", "docs", "rep"), "feat"),
        P("feat", None),
        P("feat", None),
        P(),
        P(),
        P(("groups", "docs", "rep")),
        P("groups"),
        P(("groups", "docs"), "feat"),
    )
    return jax.shard_map(
        on_device,
        mesh=mesh,
        in_specs=placed,
        out_specs=P(("groups", "rep"), ("docs", "feat")),
        check_vma=False,
    )
```

profile of v0, /device:TPU:0, one launch (start us, length us, event | category | flops | bytes accessed | tf_op | source)
XLA Modules:
  0.0 277.1 jit_solution(8919290392858870868)
XLA Ops:
  6.5 0.0 copy-start
  6.5 0.0 copy-start.3
  6.5 0.0 copy-start.4
  6.5 0.0 copy-start.1
  6.5 0.0 copy-start.2
  6.5 0.0 all-reduce.3.cloned.1.call-start
  6.6 1.2 copy-done
  7.8 4.1 %fusion.13 = f32[512,128]{1,0:T(8,128)} fusion(bf16[512,4096]{1,0:T(8,128)(2,1)} %param.9, bf16[4096,128]{1,0:T(8,128)(2,1)S(1)} %copy-done), kind=kOutput, calls=%fused_computation.32 | convolution fusion | flops 536870912 | bytes 5505024 | tf_op jit(solution)/shard_map/dot_general | solution.py:28
  11.9 4.4 %fusion.11 = f32[512,128]{1,0:T(8,128)} fusion(bf16[512,4096]{1,0:T(8,128)(2,1)} %param.10, bf16[4096,128]{1,0:T(8,128)(2,1)} %param.12), kind=kOutput, calls=%fused_computation.30 | convolution fusion | flops 536870912 | bytes 5505024 | tf_op jit(solution)/shard_map/dot_general | solution.py:29
  16.3 0.0 all-reduce.3.cloned.1.call-update
  16.4 0.0 reduce-scatter.3.cloned.1.call-start
  16.4 0.0 copy-done.3
  16.4 0.0 copy-done.4
  16.4 0.2 select_reduce_fusion
  16.7 31.3 %all-reduce.3.cloned.1.call-done = (f32[512,128]{1,0:T(8,128)}, f32[512,128]{1,0:T(8,128)}) async-done(((f32[512,128]{1,0:T(8,128)}, f32[512,128]{1,0:T(8,128)}), (f32[512,128]{1,0:T(8,128)}, f32[512,128]{1,0:T(8,128)})) %all-reduce.3.cloned.1.call-update) | async-done | bytes 524304 | tf_op jit(solution)/shard_map/psum | solution.py:30
  48.0 0.0 copy-done.1
  48.0 1.4 fusion.12
  49.4 0.1 copy.11
  49.5 0.0 copy-done.2
  49.5 1.3 fusion.14
  50.8 6.6 %multiply_convert_fusion = bf16[512,64,128]{2,1,0:T(8,128)(2,1)S(1)} fusion(f32[512,128]{1,0:T(8,128)S(1)} %fusion.14, f32[512,64]{1,0:T(8,128)S(1)} %copy.11), kind=kLoop, calls=%fused_computation | loop fusion | flops 8388608 | bytes 8781824 | tf_op jit(solution)/shard_map/convert_element_type | solution.py:12
  57.4 21.5 %convolution_convert_fusion = bf16[512,8192]{1,0:T(8,128)(2,1)} fusion(bf16[64,8,64,128]{3,2,1,0:T(8,128)(2,1)S(1)} %bitcast.14, s32[512]{0:T(512)S(1)} %fusion.6), kind=kOutput, calls=%fused_computation.1 | convolution fusion | flops 4299423744 | bytes 16779264 | tf_op jit(solution)/shard_map/dot_general | solution.py:48
  78.9 0.0 reduce-scatter.3.cloned.1.call-update
  78.9 0.0 all-gather.2.cloned.1.call-start
  79.0 89.7 %reduce-scatter.3.cloned.1.call-done = bf16[64,8192]{1,0:T(8,128)(2,1)} async-done(((bf16[512,8192]{1,0:T(8,128)(2,1)}), bf16[64,8192]{1,0:T(8,128)(2,1)}) %reduce-scatter.3.cloned.1.call-update) | async-done | bytes 1048592 | tf_op jit(solution)/shard_map/reduce_scatter | solution.py:53
  168.7 0.0 all-gather.2.cloned.1.call-update
  168.7 0.2 reduce-scatter.5.cloned.1.call-start
  169.0 80.5 %all-gather.2.cloned.1.call-done = bf16[256,8192]{1,0:T(8,128)(2,1)} async-done(((bf16[64,8192]{1,0:T(8,128)(2,1)}), bf16[256,8192]{1,0:T(8,128)(2,1)}) %all-gather.2.cloned.1.call-update) | async-done | bytes 4194320 | tf_op jit(solution)/shard_map/all_gather | solution.py:56
  249.5 7.8 %fusion.15 = f32[256,512]{1,0:T(8,128)} fusion(bf16[256,8192]{1,0:T(8,128)(2,1)} %all-gather.2.cloned.1.call-done, bf16[512,8192]{1,0:T(8,128)(2,1)} %param.17), kind=kOutput, calls=%fused_computation.34 | convolution fusion | flops 2147483648 | bytes 13107200 | tf_op jit(solution)/shard_map/dot_general | solution.py:16
  257.3 0.0 reduce-scatter.5.cloned.1.call-update
  257.4 13.2 %reduce-scatter.5.cloned.1.call-done = f32[256,256]{1,0:T(8,128)} async-done(((f32[256,512]{1,0:T(8,128)}), f32[256,256]{1,0:T(8,128)}) %reduce-scatter.5.cloned.1.call-update) | async-done | bytes 262160 | tf_op jit(solution)/shard_map/reduce_scatter | solution.py:57
  (2 shorter events, 0.0 us)
Async XLA Ops:
  6.5 1.2 copy-start
  6.5 9.9 %copy-start.3 = (s32[512]{0:T(512)S(1)}, s32[512]{0:T(512)}, u32[]{:S(2)}) copy-start(s32[512]{0:T(512)} %param.16) | copy-start | bytes 6148
  6.5 9.9 %copy-start.4 = (s32[512]{0:T(512)S(1)}, s32[512]{0:T(512)}, u32[]{:S(2)}) copy-start(s32[512]{0:T(512)} %param.15) | copy-start | bytes 6148
  6.5 41.4 %copy-start.1 = (f32[128,128]{1,0:T(8,128)S(1)}, f32[128,128]{1,0:T(8,128)}, u32[]{:S(2)}) copy-start(f32[128,128]{1,0:T(8,128)} %param.14) | copy-start | bytes 196612
  6.5 43.0 %copy-start.2 = (f32[128,128]{1,0:T(8,128)S(1)}, f32[128,128]{1,0:T(8,128)}, u32[]{:S(2)}) copy-start(f32[128,128]{1,0:T(8,128)} %param.13) | copy-start | bytes 196612
  6.5 41.4 %all-reduce.3.cloned.1.call-start = ((), (), s32[]{:S(2)}) async-start(), calls=%async_computation.5 | async-start | bytes 1048576 | tf_op jit(solution)/shard_map/psum | solution.py:30
  16.4 152.4 %reduce-scatter.3.cloned.1.call-start = ((), (), s32[]{:S(2)}) async-start(), calls=%async_computation.2 | async-start | bytes 9437184 | tf_op jit(solution)/shard_map/reduce_scatter | solution.py:53
  78.9 170.6 %all-gather.2.cloned.1.call-start = ((), (), s32[]{:S(2)}) async-start(), calls=%async_computation.3 | async-start | bytes 5242880 | tf_op jit(solution)/shard_map/all_gather | solution.py:56
  168.7 101.8 %reduce-scatter.5.cloned.1.call-start = ((), (), s32[]{:S(2)}) async-start(), calls=%async_computation.4 | async-start | bytes 786432 | tf_op jit(solution)/shard_map/reduce_scatter | solution.py:57
Sparse Core Ops, SparseCore 0:
  16.5 31.4 all-reduce.2
  79.1 89.6 reduce-scatter.2
  170.4 79.0 all-gather.1
  257.5 13.0 reduce-scatter.4
where the time goes:
time: 277 us
  waiting for transfers between devices  215 us (78%)
  matrix products  40.6 us (15%)
  between operations  13.2 us (5%)
  other arithmetic  6.85 us (2%)
    reduce_scatter x1, waiting for transfers between devices, on_device(): lax.psum_scatter(partial_terms.astype(jnp.bfloat16), ('docs', 'rep'), sca...  89.7 us
    all_gather x1, waiting for transfers between devices, on_device(): lax.all_gather(blocks, 'docs', axis=0, tiled=True)  80.5 us
    psum x1, waiting for transfers between devices, on_device(): summed_in, summed_out = lax.psum((part_in, part_out), 'feat')  31.3 us
    dot_general x1, matrix products, on_device(): lax.dot_general(onehot, products, (((0,), (0,)), ((), ())), preferred_ele...  21.5 us
    reduce_scatter x1, waiting for transfers between devices, on_device(): lax.psum_scatter(partial_scores, 'feat', scatter_dimension=1, tiled=True)  13.2 us
    dot_general x1, matrix products, score_rows(): lax.dot_general(panel_rows, stored, (((1,), (1,)), ((), ())), preferred_e...  7.83 us
    convert_element_type x1, other arithmetic, outer_rows(): joined.reshape(count, side_g.shape[1] * side_x.shape[1])  6.58 us
  transfers between devices with their start and end apart: 4, of which 4 were waited for; matrix products, arithmetic and copies ran while one was open for 0% of the time, Pallas kernels for 0%

commit v1 on v0

v1 whole, which is shorter than its diff:
```python
import functools
import jax
import jax.numpy as jnp
from jax import lax
from jax.experimental import pallas as pl
from jax.experimental.pallas import tpu as pltpu
from jax.sharding import PartitionSpec as P

QUERIES = 512
ROWS = 16
MESH = pl.DeviceIdType.MESH
F32, BF16 = jnp.float32, jnp.bfloat16


def flipped(me, step, count):
    if count & (count - 1):
        return lax.rem(me + step, count), lax.rem(me + count - step, count)
    other, bit = me, 1
    while bit < count:
        if step & bit:
            other = other + (1 - 2 * lax.rem(me // bit, 2)) * bit
        bit *= 2
    return other, other


def kernel(
    n_feat, n_docs, n_rep,
    act, grads, pin, pout, inv_in, inv_out, seg, owner, stored, out,
    act_v, grads_v, pin_v, pout_v, st_v,
    g_own, x_own, x_send, g_send, x_recv, g_recv, all_x, all_g, totals, acc,
    rep_recv, feat_send, feat_recv,
    load_sem, xs_sem, xr_sem, gs_sem, gr_sem, axs_sem, axr_sem, ags_sem, agr_sem,
    rs_sem, rr_sem, fs_sem, fr_sem,
):
    tokens = act.shape[0]
    width = inv_in.shape[0]
    side = width // n_feat
    half_tok = tokens // 2
    half_q = QUERIES // n_rep
    doc_rows = stored.shape[0] // n_feat
    feat, docs, rep = lax.axis_index("feat"), lax.axis_index("docs"), lax.axis_index("rep")

    def load(src, dst, index):
        return pltpu.make_async_copy(src, dst, load_sem.at[index])

    loads = [load(pin, pin_v, 0)]
    for i in range(2):
        rows = pl.ds(i * half_tok, half_tok)
        loads.append(load(act.at[rows], act_v.at[rows], 1 + i))
    loads.append(load(pout, pout_v, 3))
    for i in range(2):
        rows = pl.ds(i * half_tok, half_tok)
        loads.append(load(grads.at[rows], grads_v.at[rows], 4 + i))
    loads.append(load(stored, st_v, 6))
    for one in loads:
        one.start()

    barrier = pltpu.get_barrier_semaphore()
    feat_to = [flipped(feat, j, n_feat)[0] for j in range(n_feat)]
    docs_to = [flipped(docs, j, n_docs)[0] for j in range(n_docs)]
    rep_to = [flipped(rep, j, n_rep)[0] for j in range(n_rep)]
    for name, peers in (("feat", feat_to), ("docs", docs_to), ("rep", rep_to)):
        for peer in peers[1:]:
            pl.semaphore_signal(barrier, inc=1, device_id={name: peer}, device_id_type=MESH)

    seg_count = owner.shape[1]
    hit = lax.broadcasted_iota(jnp.int32, (seg_count, tokens), 0) == seg[...]
    hit = jnp.where(hit, 1.0, 0.0).astype(BF16)
    owners = owner[...]
    high = lax.div(owners, ROWS)
    low = owners - high * ROWS
    row = lax.broadcasted_iota(jnp.int32, (ROWS, seg_count), 0)
    digits = jnp.where(row == 0, high, jnp.where(row == 1, low, 0)).astype(F32).astype(BF16)
    all_g[0, side:, :] = jnp.dot(digits, hit, preferred_element_type=F32).astype(BF16)

    pl.semaphore_wait(barrier, (n_feat - 1) + (n_docs - 1) + (n_rep - 1))

    def send(src, dst, s_sem, r_sem, name, peer):
        return pltpu.make_async_remote_copy(
            src_ref=src, dst_ref=dst, send_sem=s_sem, recv_sem=r_sem,
            device_id={name: peer}, device_id_type=MESH,
        )

    def conditioned(values, proj_v, inv, first):
        parts = []
        for i in range(2):
            loads[first + i].wait()
            parts.append(jnp.dot(
                values[i * half_tok:(i + 1) * half_tok, :], proj_v[...], preferred_element_type=F32
            ))
        part = jnp.concatenate(parts, axis=0)
        return jnp.dot(
            part, inv[...], precision=lax.Precision.HIGHEST, preferred_element_type=F32
        ).T

    loads[0].wait()
    x_own[...] = conditioned(act_v, pin_v, inv_in, 1)
    x_send[...] = x_own[...].astype(BF16)
    x_copies, g_copies = [], []
    for j in range(1, n_feat):
        copy = send(x_send, x_recv.at[j], xs_sem.at[j], xr_sem.at[j], "feat", feat_to[j])
        copy.start()
        x_copies.append(copy)

    loads[3].wait()
    g_own[...] = conditioned(grads_v, pout_v, inv_out, 4)
    for j in range(1, n_feat):
        rows = pl.ds(pl.multiple_of(feat_to[j] * side, side), side)
        g_send[j] = g_own[rows, :].astype(BF16)
        copy = send(g_send.at[j], g_recv.at[j], gs_sem.at[j], gr_sem.at[j], "feat", feat_to[j])
        copy.start()
        g_copies.append(copy)

    x_sum = x_own[...]
    for j in range(1, n_feat):
        x_copies[j - 1].wait_recv()
        x_sum = x_sum + x_recv[j].astype(F32)
    all_x[0] = x_sum.astype(BF16)
    ax_copies, ag_copies = [], []
    for j in range(1, n_docs):
        copy = send(all_x.at[0], all_x.at[j], axs_sem.at[j], axr_sem.at[j], "docs", docs_to[j])
        copy.start()
        ax_copies.append(copy)
    g_sum = g_own[pl.ds(pl.multiple_of(feat * side, side), side), :]
    for j in range(1, n_feat):
        g_copies[j - 1].wait_recv()
        g_sum = g_sum + g_recv[j].astype(F32)
    all_g[0, :side, :] = g_sum.astype(BF16)
    for j in range(1, n_docs):
        copy = send(all_g.at[0], all_g.at[j], ags_sem.at[j], agr_sem.at[j], "docs", docs_to[j])
        copy.start()
        ag_copies.append(copy)

    loads[6].wait()
    acc[...] = jnp.zeros_like(acc)

    def shard(step, carry):
        @pl.when(step > 0)
        def _():
            send(all_x.at[0], all_x.at[step], axs_sem.at[step], axr_sem.at[step], "docs", docs_to[-1]).wait_recv()
            send(all_g.at[0], all_g.at[step], ags_sem.at[step], agr_sem.at[step], "docs", docs_to[-1]).wait_recv()

        totals[...] = jnp.zeros_like(totals)

        def chunk(c, inner):
            x = all_x[step].reshape(width // ROWS, ROWS, tokens)
            g = all_g[step, pl.ds(pl.multiple_of(c * ROWS, ROWS), ROWS), :].astype(F32)
            outer = []
            for j in range(ROWS):
                line = jnp.broadcast_to(g[j:j + 1, :], (ROWS, tokens)).astype(BF16)
                outer.append((x * line[None]).reshape(width, tokens))
            outer = jnp.concatenate(outer, axis=0)
            cols = pl.ds(pl.multiple_of(c * ROWS * width, ROWS * width), ROWS * width)
            totals[...] += jnp.dot(st_v[:, cols], outer, preferred_element_type=F32)
            return inner

        lax.fori_loop(0, side // ROWS, chunk, 0)
        digit = all_g[step, side:, :].astype(F32)
        query = (digit[0:1, :] * ROWS + digit[1:2, :]).astype(jnp.int32)
        mine = lax.broadcasted_iota(jnp.int32, (QUERIES, tokens), 0) == query
        mine = jnp.where(mine, 1.0, 0.0).astype(BF16)
        for f in range(n_feat):
            rows = totals[f * doc_rows:(f + 1) * doc_rows, :].astype(BF16)
            acc[f] += lax.dot_general(
                mine, rows, (((1,), (1,)), ((), ())), preferred_element_type=F32
            )
        return carry

    lax.fori_loop(0, n_docs, shard, 0)

    r_copies = []
    for j in range(1, n_rep):
        rows = pl.ds(pl.multiple_of(rep_to[j] * half_q, half_q), half_q)
        copy = send(acc.at[:, rows, :], rep_recv.at[j], rs_sem.at[j], rr_sem.at[j], "rep", rep_to[j])
        copy.start()
        r_copies.append(copy)
    for copy in r_copies:
        copy.wait_recv()
    own = pl.ds(pl.multiple_of(rep * half_q, half_q), half_q)

    def over_rep(f):
        value = acc[f, own, :]
        for j in range(1, n_rep):
            value = value + rep_recv[j, f]
        return value

    f_copies = []
    for j in range(1, n_feat):
        feat_send[j] = over_rep(feat_to[j]).astype(BF16)
        copy = send(feat_send.at[j], feat_recv.at[j], fs_sem.at[j], fr_sem.at[j], "feat", feat_to[j])
        copy.start()
        f_copies.append(copy)
    value = over_rep(feat)
    for j in range(1, n_feat):
        f_copies[j - 1].wait_recv()
        value = value + feat_recv[j].astype(F32)
    out[...] = value
    for copy in x_copies + g_copies + ax_copies + ag_copies + r_copies + f_copies:
        copy.wait_send()


def on_device(
    n_feat, n_docs, n_rep,
    activations, out_grads, proj_in, proj_out, inv_in, inv_out, segment_ids, owner_map, stored
):
    tokens = activations.shape[0]
    width = inv_in.shape[0]
    side = width // n_feat
    n_stored = stored.shape[0]
    doc_rows = n_stored // n_feat
    half_q = QUERIES // n_rep
    dma = pltpu.SemaphoreType.DMA
    anywhere = pl.BlockSpec(memory_space=pl.ANY)
    vmem = pl.BlockSpec(memory_space=pltpu.VMEM)
    return pl.pallas_call(
        functools.partial(kernel, n_feat, n_docs, n_rep),
        out_shape=jax.ShapeDtypeStruct((half_q, doc_rows), F32),
        in_specs=[anywhere] * 4 + [vmem] * 4 + [anywhere],
        out_specs=vmem,
        scratch_shapes=[
            pltpu.VMEM(activations.shape, BF16),
            pltpu.VMEM(out_grads.shape, BF16),
            pltpu.VMEM(proj_in.shape, BF16),
            pltpu.VMEM(proj_out.shape, BF16),
            pltpu.VMEM(stored.shape, BF16),
            pltpu.VMEM((width, tokens), F32),
            pltpu.VMEM((width, tokens), F32),
            pltpu.VMEM((width, tokens), BF16),
            pltpu.VMEM((n_feat, side, tokens), BF16),
            pltpu.VMEM((n_feat, width, tokens), BF16),
            pltpu.VMEM((n_feat, side, tokens), BF16),
            pltpu.VMEM((n_docs, width, tokens), BF16),
            pltpu.VMEM((n_docs, side + ROWS, tokens), BF16),
            pltpu.VMEM((n_stored, tokens), F32),
            pltpu.VMEM((n_feat, QUERIES, doc_rows), F32),
            pltpu.VMEM((n_rep, n_feat, half_q, doc_rows), F32),
            pltpu.VMEM((n_feat, half_q, doc_rows), BF16),
            pltpu.VMEM((n_feat, half_q, doc_rows), BF16),
            dma((7,)),
            dma((n_feat,)), dma((n_feat,)), dma((n_feat,)), dma((n_feat,)),
            dma((n_docs,)), dma((n_docs,)), dma((n_docs,)), dma((n_docs,)),
            dma((n_rep,)), dma((n_rep,)), dma((n_feat,)), dma((n_feat,)),
        ],
        compiler_params=pltpu.CompilerParams(
            collective_id=0, has_side_effects=True, vmem_limit_bytes=56 * 1024 * 1024
        ),
    )(
        activations, out_grads, proj_in, proj_out, inv_in, inv_out,
        segment_ids.reshape(1, -1), owner_map.reshape(1, -1), stored,
    )


def solution(mesh):
    placed = (
        P(("groups", "docs", "rep"), "feat"),
        P(("groups", "docs", "rep"), "feat"),
        P("feat", None),
        P("feat", None),
        P(),
        P(),
        P(("groups", "docs", "rep")),
        P("groups"),
        P(("groups", "docs"), "feat"),
    )
    sizes = dict(mesh.shape)
    return jax.shard_map(
        functools.partial(on_device, sizes["feat"], sizes["docs"], sizes["rep"]),
        mesh=mesh,
        in_specs=placed,
        out_specs=P(("groups", "rep"), ("docs", "feat")),
        check_vma=False,
    )
```

time: 277 us -> 49.8 us (0.18)
  waiting for transfers between devices: 215 us -> 0 us
  Pallas kernels: 0 us -> 47.3 us
  matrix products: 40.6 us -> 0 us
  between operations: 13.2 us -> 0.01 us
  other arithmetic: 6.85 us -> 0 us
    reduce_scatter x2 -> x0, waiting for transfers between devices: 103 us -> none  [the longest x1 89.7 us: on_device(): lax.psum_scatter(partial_terms.astype(jnp.bfloat16), ('docs', 'rep'), sca...]
    all_gather x1 -> x0, waiting for transfers between devices: 80.5 us -> none  [on_device(): lax.all_gather(blocks, 'docs', axis=0, tiled=True)]
    pallas_call x0 -> x1, Pallas kernels: none -> 47.3 us  [on_device(): pl.pallas_call(functools.partial(kernel, n_feat, n_docs, n_rep), out_shap...]
    dot_general x6 -> x0, matrix products: 40.6 us -> none  [the longest x1 21.5 us: on_device(): lax.dot_general(onehot, products, (((0,), (0,)), ((), ())), preferred_ele...]
    psum x1 -> x0, waiting for transfers between devices: 31.3 us -> none  [on_device(): summed_in, summed_out = lax.psum((part_in, part_out), 'feat')]
    convert_element_type x1 -> x0, other arithmetic: 6.58 us -> none  [outer_rows(): joined.reshape(count, side_g.shape[1] * side_x.shape[1])]
  transfers between devices with their start and end apart: 4 -> 0, of which waited for: 4 -> 0; matrix products, arithmetic and copies ran while one was open for 0% -> 0% of each run, Pallas kernels for 0% -> 0%
where the time goes in v1:
time: 49.8 us; the launch traced here: 49 us
  Pallas kernels  47.3 us (95%)
  local copies, waits for them, and re-layouts  1.67 us (3%)
    pallas_call x1, Pallas kernels, on_device(): pl.pallas_call(functools.partial(kernel, n_feat, n_docs, n_rep), out_shap...  47.3 us
    unnamed x1, local copies, waits for them, and re-layouts  1.67 us

profile of v1, /device:TPU:0, one launch (start us, length us, event | category | flops | bytes accessed | tf_op | source)
XLA Modules:
  0.0 49.0 jit_solution(6090083549272383983)
XLA Ops:
  0.0 47.3 %shard_map.91 = f32[256,256]{1,0:T(8,128)} custom-call(bf16[512,4096]{1,0:T(8,128)(2,1)} %act.1, bf16[512,4096]{1,0:T(8,128)(2,1)} %grads.1, bf16[4096,128]{1,0:T(8,128)(2,1)} %pin.1, bf16[4096,128]{1,0:T(8,128)(2,1)} %pout.1, f32[128,128]{1,0:T(8,128)} %inv_in.1, f32[128,128]{1,0:T(8,128)} %inv_out.1, s32[1,512]{1,0:T(1,128)} %bitcast.2, s32[1,512]{1,0:T(1,128)} %bitcast.3, ...), custom_call_target="tpu_custom_call" | custom-call | tf_op jit(solution)/shard_map/pallas_call | solution.py:215
  47.4 1.7 %copy.11 = f32[256,256]{1,0:T(8,128)} copy(f32[256,256]{1,0:T(8,128)} %shard_map.91) | data formatting | bytes 524288

commit v2 on v1

--- a/solution.py
+++ b/solution.py
@@ -30,7 +30,7 @@
     g_own, x_own, x_send, g_send, x_recv, g_recv, all_x, all_g, totals, acc,
     rep_recv, feat_send, feat_recv,
     load_sem, xs_sem, xr_sem, gs_sem, gr_sem, axs_sem, axr_sem, ags_sem, agr_sem,
-    rs_sem, rr_sem, fs_sem, fr_sem,
+    rs_sem, rr_sem, fs_sem, fr_sem, bs_sem, br_sem,
 ):
     tokens = act.shape[0]
     width = inv_in.shape[0]
@@ -95,10 +95,11 @@
 
     loads[0].wait()
     x_own[...] = conditioned(act_v, pin_v, inv_in, 1)
-    x_send[...] = x_own[...].astype(BF16)
     x_copies, g_copies = [], []
     for j in range(1, n_feat):
-        copy = send(x_send, x_recv.at[j], xs_sem.at[j], xr_sem.at[j], "feat", feat_to[j])
+        rows = pl.ds(pl.multiple_of(feat_to[j] * side, side), side)
+        x_send[j] = x_own[rows, :].astype(BF16)
+        copy = send(x_send.at[j], x_recv.at[j], xs_sem.at[j], xr_sem.at[j], "feat", feat_to[j])
         copy.start()
         x_copies.append(copy)
 
@@ -111,17 +112,26 @@
         copy.start()
         g_copies.append(copy)
 
-    x_sum = x_own[...]
+    my_rows = pl.ds(pl.multiple_of(feat * side, side), side)
+
+    def share(step, j):
+        part = all_x.at[step, my_rows]
+        return send(part, part, bs_sem.at[step, j], br_sem.at[step, j], "feat", feat_to[j])
+
+    x_sum = x_own[my_rows, :]
     for j in range(1, n_feat):
         x_copies[j - 1].wait_recv()
         x_sum = x_sum + x_recv[j].astype(F32)
-    all_x[0] = x_sum.astype(BF16)
+    all_x[0, my_rows, :] = x_sum.astype(BF16)
     ax_copies, ag_copies = [], []
     for j in range(1, n_docs):
-        copy = send(all_x.at[0], all_x.at[j], axs_sem.at[j], axr_sem.at[j], "docs", docs_to[j])
+        part = (all_x.at[0, my_rows], all_x.at[j, my_rows])
+        copy = send(*part, axs_sem.at[j], axr_sem.at[j], "docs", docs_to[j])
         copy.start()
         ax_copies.append(copy)
-    g_sum = g_own[pl.ds(pl.multiple_of(feat * side, side), side), :]
+    for j in range(1, n_feat):
+        share(0, j).start()
+    g_sum = g_own[my_rows, :]
     for j in range(1, n_feat):
         g_copies[j - 1].wait_recv()
         g_sum = g_sum + g_recv[j].astype(F32)
@@ -135,9 +145,11 @@
     acc[...] = jnp.zeros_like(acc)
 
     def shard(step, carry):
+        for j in range(1, n_feat):
+            share(step, j).wait()
+
         @pl.when(step > 0)
         def _():
-            send(all_x.at[0], all_x.at[step], axs_sem.at[step], axr_sem.at[step], "docs", docs_to[-1]).wait_recv()
             send(all_g.at[0], all_g.at[step], ags_sem.at[step], agr_sem.at[step], "docs", docs_to[-1]).wait_recv()
 
         totals[...] = jnp.zeros_like(totals)
@@ -154,7 +166,17 @@
             totals[...] += jnp.dot(st_v[:, cols], outer, preferred_element_type=F32)
             return inner
 
-        lax.fori_loop(0, side // ROWS, chunk, 0)
+        chunks = side // ROWS
+        lax.fori_loop(0, chunks // 2, chunk, 0)
+
+        @pl.when(step + 1 < n_docs)
+        def _():
+            part = (all_x.at[0, my_rows], all_x.at[step + 1, my_rows])
+            send(*part, axs_sem.at[step + 1], axr_sem.at[step + 1], "docs", docs_to[-1]).wait_recv()
+            for j in range(1, n_feat):
+                share(step + 1, j).start()
+
+        lax.fori_loop(chunks // 2, chunks, chunk, 0)
         digit = all_g[step, side:, :].astype(F32)
         query = (digit[0:1, :] * ROWS + digit[1:2, :]).astype(jnp.int32)
         mine = lax.broadcasted_iota(jnp.int32, (QUERIES, tokens), 0) == query
@@ -225,9 +247,9 @@
             pltpu.VMEM(stored.shape, BF16),
             pltpu.VMEM((width, tokens), F32),
             pltpu.VMEM((width, tokens), F32),
-            pltpu.VMEM((width, tokens), BF16),
-            pltpu.VMEM((n_feat, side, tokens), BF16),
-            pltpu.VMEM((n_feat, width, tokens), BF16),
+            pltpu.VMEM((n_feat, side, tokens), BF16),
+            pltpu.VMEM((n_feat, side, tokens), BF16),
+            pltpu.VMEM((n_feat, side, tokens), BF16),
             pltpu.VMEM((n_feat, side, tokens), BF16),
             pltpu.VMEM((n_docs, width, tokens), BF16),
             pltpu.VMEM((n_docs, side + ROWS, tokens), BF16),
@@ -240,6 +262,7 @@
             dma((n_feat,)), dma((n_feat,)), dma((n_feat,)), dma((n_feat,)),
             dma((n_docs,)), dma((n_docs,)), dma((n_docs,)), dma((n_docs,)),
             dma((n_rep,)), dma((n_rep,)), dma((n_feat,)), dma((n_feat,)),
+            dma((n_docs, n_feat)), dma((n_docs, n_feat)),
         ],
         compiler_params=pltpu.CompilerParams(
             collective_id=0, has_side_effects=True, vmem_limit_bytes=56 * 1024 * 1024

time: 49.8 us -> 45.8 us (0.920)
  Pallas kernels: 47.3 us -> 43.3 us
    pallas_call x1, Pallas kernels: 47.3 us -> 43.3 us  [on_device(): pl.pallas_call(functools.partial(kernel, n_feat, n_docs, n_rep), out_shap...]
where the time goes in v2:
time: 45.8 us; the launch traced here: 45 us
  Pallas kernels  43.3 us (95%)
  local copies, waits for them, and re-layouts  1.67 us (4%)
    pallas_call x1, Pallas kernels, on_device(): pl.pallas_call(functools.partial(kernel, n_feat, n_docs, n_rep), out_shap...  43.3 us
    unnamed x1, local copies, waits for them, and re-layouts  1.67 us

profile of v2, /device:TPU:0, one launch (start us, length us, event | category | flops | bytes accessed | tf_op | source)
XLA Modules:
  0.0 45.0 jit_solution(9001919792669120454)
XLA Ops:
  0.0 43.3 %shard_map.91 = f32[256,256]{1,0:T(8,128)} custom-call(bf16[512,4096]{1,0:T(8,128)(2,1)} %act.1, bf16[512,4096]{1,0:T(8,128)(2,1)} %grads.1, bf16[4096,128]{1,0:T(8,128)(2,1)} %pin.1, bf16[4096,128]{1,0:T(8,128)(2,1)} %pout.1, f32[128,128]{1,0:T(8,128)} %inv_in.1, f32[128,128]{1,0:T(8,128)} %inv_out.1, s32[1,512]{1,0:T(1,128)} %bitcast.2, s32[1,512]{1,0:T(1,128)} %bitcast.3, ...), custom_call_target="tpu_custom_call" | custom-call | tf_op jit(solution)/shard_map/pallas_call | solution.py:237
  43.3 1.7 %copy.11 = f32[256,256]{1,0:T(8,128)} copy(f32[256,256]{1,0:T(8,128)} %shard_map.91) | data formatting | bytes 524288

commit v3 on v2

--- a/solution.py
+++ b/solution.py
@@ -8,6 +8,7 @@
 
 QUERIES = 512
 ROWS = 16
+CUTS = 4
 MESH = pl.DeviceIdType.MESH
 F32, BF16 = jnp.float32, jnp.bfloat16
 
@@ -35,7 +36,7 @@
     tokens = act.shape[0]
     width = inv_in.shape[0]
     side = width // n_feat
-    half_tok = tokens // 2
+    cut = act.shape[1] // CUTS
     half_q = QUERIES // n_rep
     doc_rows = stored.shape[0] // n_feat
     feat, docs, rep = lax.axis_index("feat"), lax.axis_index("docs"), lax.axis_index("rep")
@@ -44,14 +45,14 @@
         return pltpu.make_async_copy(src, dst, load_sem.at[index])
 
     loads = [load(pin, pin_v, 0)]
-    for i in range(2):
-        rows = pl.ds(i * half_tok, half_tok)
-        loads.append(load(act.at[rows], act_v.at[rows], 1 + i))
-    loads.append(load(pout, pout_v, 3))
-    for i in range(2):
-        rows = pl.ds(i * half_tok, half_tok)
-        loads.append(load(grads.at[rows], grads_v.at[rows], 4 + i))
-    loads.append(load(stored, st_v, 6))
+    for i in range(CUTS):
+        cols = pl.ds(i * cut, cut)
+        loads.append(load(act.at[:, cols], act_v.at[:, cols], 1 + i))
+    loads.append(load(pout, pout_v, 1 + CUTS))
+    for i in range(CUTS):
+        cols = pl.ds(i * cut, cut)
+        loads.append(load(grads.at[:, cols], grads_v.at[:, cols], 2 + CUTS + i))
+    loads.append(load(stored, st_v, 2 + 2 * CUTS))
     for one in loads:
         one.start()
 
@@ -73,8 +74,6 @@
     digits = jnp.where(row == 0, high, jnp.where(row == 1, low, 0)).astype(F32).astype(BF16)
     all_g[0, side:, :] = jnp.dot(digits, hit, preferred_element_type=F32).astype(BF16)
 
-    pl.semaphore_wait(barrier, (n_feat - 1) + (n_docs - 1) + (n_rep - 1))
-
     def send(src, dst, s_sem, r_sem, name, peer):
         return pltpu.make_async_remote_copy(
             src_ref=src, dst_ref=dst, send_sem=s_sem, recv_sem=r_sem,
@@ -82,19 +81,19 @@
         )
 
     def conditioned(values, proj_v, inv, first):
-        parts = []
-        for i in range(2):
+        part = None
+        for i in range(CUTS):
             loads[first + i].wait()
-            parts.append(jnp.dot(
-                values[i * half_tok:(i + 1) * half_tok, :], proj_v[...], preferred_element_type=F32
-            ))
-        part = jnp.concatenate(parts, axis=0)
+            cols = slice(i * cut, (i + 1) * cut)
+            more = jnp.dot(values[:, cols], proj_v[cols, :], preferred_element_type=F32)
+            part = more if part is None else part + more
         return jnp.dot(
             part, inv[...], precision=lax.Precision.HIGHEST, preferred_element_type=F32
         ).T
 
     loads[0].wait()
     x_own[...] = conditioned(act_v, pin_v, inv_in, 1)
+    pl.semaphore_wait(barrier, (n_feat - 1) + (n_docs - 1) + (n_rep - 1))
     x_copies, g_copies = [], []
     for j in range(1, n_feat):
         rows = pl.ds(pl.multiple_of(feat_to[j] * side, side), side)
@@ -103,8 +102,8 @@
         copy.start()
         x_copies.append(copy)
 
-    loads[3].wait()
-    g_own[...] = conditioned(grads_v, pout_v, inv_out, 4)
+    loads[1 + CUTS].wait()
+    g_own[...] = conditioned(grads_v, pout_v, inv_out, 2 + CUTS)
     for j in range(1, n_feat):
         rows = pl.ds(pl.multiple_of(feat_to[j] * side, side), side)
         g_send[j] = g_own[rows, :].astype(BF16)
@@ -141,10 +140,12 @@
         copy.start()
         ag_copies.append(copy)
 
-    loads[6].wait()
+    loads[2 + 2 * CUTS].wait()
     acc[...] = jnp.zeros_like(acc)
 
-    def shard(step, carry):
+    chunks = side // ROWS
+
+    def arrive(step):
         for j in range(1, n_feat):
             share(step, j).wait()
 
@@ -152,8 +153,13 @@
         def _():
             send(all_g.at[0], all_g.at[step], ags_sem.at[step], agr_sem.at[step], "docs", docs_to[-1]).wait_recv()
 
-        totals[...] = jnp.zeros_like(totals)
-
+    def forward(step):
+        part = (all_x.at[0, my_rows], all_x.at[step, my_rows])
+        send(*part, axs_sem.at[step], axr_sem.at[step], "docs", docs_to[-1]).wait_recv()
+        for j in range(1, n_feat):
+            share(step, j).start()
+
+    def multiply(step, rows, first, last):
         def chunk(c, inner):
             x = all_x[step].reshape(width // ROWS, ROWS, tokens)
             g = all_g[step, pl.ds(pl.multiple_of(c * ROWS, ROWS), ROWS), :].astype(F32)
@@ -163,61 +169,87 @@
                 outer.append((x * line[None]).reshape(width, tokens))
             outer = jnp.concatenate(outer, axis=0)
             cols = pl.ds(pl.multiple_of(c * ROWS * width, ROWS * width), ROWS * width)
-            totals[...] += jnp.dot(st_v[:, cols], outer, preferred_element_type=F32)
+            totals[rows, :] += jnp.dot(st_v[rows, cols], outer, preferred_element_type=F32)
             return inner
 
-        chunks = side // ROWS
-        lax.fori_loop(0, chunks // 2, chunk, 0)
-
-        @pl.when(step + 1 < n_docs)
-        def _():
-            part = (all_x.at[0, my_rows], all_x.at[step + 1, my_rows])
-            send(*part, axs_sem.at[step + 1], axr_sem.at[step + 1], "docs", docs_to[-1]).wait_recv()
-            for j in range(1, n_feat):
-                share(step + 1, j).start()
-
-        lax.fori_loop(chunks // 2, chunks, chunk, 0)
+        lax.fori_loop(first, last, chunk, 0)
+
+    def owned(step):
         digit = all_g[step, side:, :].astype(F32)
         query = (digit[0:1, :] * ROWS + digit[1:2, :]).astype(jnp.int32)
         mine = lax.broadcasted_iota(jnp.int32, (QUERIES, tokens), 0) == query
-        mine = jnp.where(mine, 1.0, 0.0).astype(BF16)
+        return jnp.where(mine, 1.0, 0.0).astype(BF16)
+
+    def gather(mine, f, rows):
+        acc[f] += lax.dot_general(
+            mine, totals[rows, :].astype(BF16), (((1,), (1,)), ((), ())),
+            preferred_element_type=F32,
+        )
+
+    def shard(step, carry):
+        arrive(step)
+        totals[...] = jnp.zeros_like(totals)
+        whole = pl.ds(0, n_feat * doc_rows)
+        multiply(step, whole, 0, chunks // 2)
+        forward(step + 1)
+        multiply(step, whole, chunks // 2, chunks)
+        mine = owned(step)
         for f in range(n_feat):
-            rows = totals[f * doc_rows:(f + 1) * doc_rows, :].astype(BF16)
-            acc[f] += lax.dot_general(
-                mine, rows, (((1,), (1,)), ((), ())), preferred_element_type=F32
-            )
+            gather(mine, f, pl.ds(f * doc_rows, doc_rows))
         return carry
 
-    lax.fori_loop(0, n_docs, shard, 0)
-
-    r_copies = []
-    for j in range(1, n_rep):
-        rows = pl.ds(pl.multiple_of(rep_to[j] * half_q, half_q), half_q)
-        copy = send(acc.at[:, rows, :], rep_recv.at[j], rs_sem.at[j], rr_sem.at[j], "rep", rep_to[j])
-        copy.start()
-        r_copies.append(copy)
-    for copy in r_copies:
-        copy.wait_recv()
+    lax.fori_loop(0, n_docs - 2, shard, 0)
+
+    def slice_of(step, i, fresh):
+        rows = pl.ds(pl.multiple_of(feat_to[i] * doc_rows, doc_rows), doc_rows)
+        totals[rows, :] = jnp.zeros((doc_rows, tokens), F32)
+        if fresh:
+            arrive(step)
+        multiply(step, rows, 0, chunks // 2)
+        if fresh and step + 1 < n_docs:
+            forward(step + 1)
+        multiply(step, rows, chunks // 2, chunks)
+        gather(owned(step), feat_to[i], rows)
+
+    r_copies, f_copies = [], []
+
+    def to_rep(i):
+        for j in range(1, n_rep):
+            rows = pl.ds(pl.multiple_of(rep_to[j] * half_q, half_q), half_q)
+            part = (acc.at[feat_to[i], rows], rep_recv.at[j, feat_to[i]])
+            copy = send(*part, rs_sem.at[j, i], rr_sem.at[j, i], "rep", rep_to[j])
+            copy.start()
+            r_copies.append((i, copy))
+
     own = pl.ds(pl.multiple_of(rep * half_q, half_q), half_q)
 
-    def over_rep(f):
-        value = acc[f, own, :]
+    def over_rep(i):
+        for at, copy in r_copies:
+            if at == i:
+                copy.wait_recv()
+        value = acc[feat_to[i], own, :]
         for j in range(1, n_rep):
-            value = value + rep_recv[j, f]
+            value = value + rep_recv[j, feat_to[i]]
         return value
 
-    f_copies = []
-    for j in range(1, n_feat):
-        feat_send[j] = over_rep(feat_to[j]).astype(BF16)
+    for i in range(1, n_feat):
+        for step in range(n_docs - 2, n_docs):
+            slice_of(step, i, i == 1)
+        to_rep(i)
+    slice_of(n_docs - 2, 0, False)
+    for j in range(1, n_feat):
+        feat_send[j] = over_rep(j).astype(BF16)
         copy = send(feat_send.at[j], feat_recv.at[j], fs_sem.at[j], fr_sem.at[j], "feat", feat_to[j])
         copy.start()
         f_copies.append(copy)
-    value = over_rep(feat)
+    slice_of(n_docs - 1, 0, False)
+    to_rep(0)
+    value = over_rep(0)
     for j in range(1, n_feat):
         f_copies[j - 1].wait_recv()
         value = value + feat_recv[j].astype(F32)
     out[...] = value
-    for copy in x_copies + g_copies + ax_copies + ag_copies + r_copies + f_copies:
+    for copy in x_copies + g_copies + ax_copies + ag_copies + [c for _, c in r_copies] + f_copies:
         copy.wait_send()
 
 
@@ -258,10 +290,10 @@
             pltpu.VMEM((n_rep, n_feat, half_q, doc_rows), F32),
             pltpu.VMEM((n_feat, half_q, doc_rows), BF16),
             pltpu.VMEM((n_feat, half_q, doc_rows), BF16),
-            dma((7,)),
+            dma((3 + 2 * CUTS,)),
             dma((n_feat,)), dma((n_feat,)), dma((n_feat,)), dma((n_feat,)),
             dma((n_docs,)), dma((n_docs,)), dma((n_docs,)), dma((n_docs,)),
-            dma((n_rep,)), dma((n_rep,)), dma((n_feat,)), dma((n_feat,)),
+            dma((n_rep, n_feat)), dma((n_rep, n_feat)), dma((n_feat,)), dma((n_feat,)),
             dma((n_docs, n_feat)), dma((n_docs, n_feat)),
         ],
         compiler_params=pltpu.CompilerParams(

time: 45.8 us -> 45.2 us (0.987); the launches traced: 45 us -> 45 us
  no operation moved by 1% of the time
where the time goes in v3:
time: 45.2 us; the launch traced here: 45 us
  Pallas kernels  43.3 us (96%)
  local copies, waits for them, and re-layouts  1.67 us (4%)
    pallas_call x1, Pallas kernels, on_device(): pl.pallas_call(functools.partial(kernel, n_feat, n_docs, n_rep), out_shap...  43.3 us
    unnamed x1, local copies, waits for them, and re-layouts  1.67 us

profile of v3, /device:TPU:0, one launch (start us, length us, event | category | flops | bytes accessed | tf_op | source)
XLA Modules:
  0.0 45.0 jit_solution(11141650974793504539)
XLA Ops:
  0.0 43.3 %shard_map.91 = f32[256,256]{1,0:T(8,128)} custom-call(bf16[512,4096]{1,0:T(8,128)(2,1)} %act.1, bf16[512,4096]{1,0:T(8,128)(2,1)} %grads.1, bf16[4096,128]{1,0:T(8,128)(2,1)} %pin.1, bf16[4096,128]{1,0:T(8,128)(2,1)} %pout.1, f32[128,128]{1,0:T(8,128)} %inv_in.1, f32[128,128]{1,0:T(8,128)} %inv_out.1, s32[1,512]{1,0:T(1,128)} %bitcast.2, s32[1,512]{1,0:T(1,128)} %bitcast.3, ...), custom_call_target="tpu_custom_call" | custom-call | tf_op jit(solution)/shard_map/pallas_call | solution.py:269
  43.4 1.7 %copy.11 = f32[256,256]{1,0:T(8,128)} copy(f32[256,256]{1,0:T(8,128)} %shard_map.91) | data formatting | bytes 524288
